TPU v7x, 32 devices: a whole 2x2x4 slice. The times are simulated.
32 devices in a mesh: ens: 2 (over y), space: 4 (over z), chan: 2 (over x), sub: 2 (over core).
Axes of the slice: x: 2, y: 2, z: 4, core: 2. Of those that a mesh axis runs over, the one named last changes fastest.
Arguments:
- state_tiles: bfloat16 [128, 16, 128, 128], P(('ens', 'space'), None, ('chan', 'sub')), parts along dimension 0, may hold values from -6 to 6
- water_mask: int32 [64], replicated, may hold values from 0 to 1, as said below
- owner_tiles: int32 [4, 8], replicated, may hold values from 0 to 63, as said below
- neighbors: int32 [64, 3], replicated, may hold values from 0 to 64, as said below
- first_kernel: bfloat16 [3, 3, 16, 256], replicated, may hold values from -0.5 to 0.5
- second_kernel: bfloat16 [3, 3, 256, 512], replicated, may hold values from -0.125 to 0.125
- mix_kernel: bfloat16 [512, 512], P(None, ('chan', 'sub')), may hold values from -0.25 to 0.25
Outputs:
- mixed_out: bfloat16 [64, 32, 32, 512], P(('ens', 'space'), ('chan', 'sub')), parts along dimension 0
There are 2 independent parts, one for each index of `ens`. A program takes and returns all parts, laid end to end along the dimension named above; an argument that names none is the same for every part. Nothing has to cross between parts.
Inputs may be any that keep to these rules, and one draw needn't show every extreme that they name: `water_mask`: exactly 30 tiles are water; all 16 tiles held by one index of space are water. `owner_tiles`: every water tile stands in exactly one slot; the other slots hold a land tile. Each owner holds 7 or 8 water tiles, half of the owners exactly 8. Tile t is held on entry by index t // 16 of space; no owner receives more than 4 water tiles from one such index, and some owner receives exactly 4. `neighbors`: tiles lie on a rectangular grid; 64 stands where a tile lies on the grid's edge and has no such neighbor.
All inputs are finite; a program needn't handle non-finite values.
Results may differ from a plain program's by a relative error of at most 0.0058.
Values may be sent and summed in bfloat16 or wider, within the bound.
A program may use at most 128 MiB of HBM per device.

v0:
```python
import functools

import jax
import jax.numpy as jnp
import numpy as np
from jax import lax
from jax.experimental import pallas as pl
from jax.experimental.pallas import tpu as pltpu
from jax.sharding import PartitionSpec as P

BF16 = jnp.bfloat16
F32 = jnp.float32
REACH = 3
WINDOW = 8


def exact(spec, one_hot, values):
    return jnp.einsum(spec, one_hot, values, preferred_element_type=F32).astype(BF16)


def column_picker(width, slots):
    lanes = 128
    used = (lanes // (REACH * slots)) * REACH * slots
    count = width // 4
    picks = np.zeros((3, 3, count, lanes + width), np.float32)
    for tap in range(3):
        for kind in range(3):
            for at in range(count):
                col = 4 * at - 3 + 2 * kind + tap
                if col >= 0:
                    picks[tap, kind, at, lanes + col] = 1
                else:
                    picks[tap, kind, at, np.arange(col + REACH, used, REACH)] = 1
    return picks.reshape(9 * count, lanes + width)


def silu(x):
    return x * (1.0 / (1.0 + jnp.exp(-x)))


def tile_kernel(
    slots,
    table,
    slab_ref,
    halo_ref,
    picks_ref,
    first_ref,
    second_ref,
    mix_ref,
    out_ref,
    raw,
    maps,
):
    k = pl.program_id(0)
    rows, chans, width = slab_ref.shape[1:]
    blocks = rows // 4
    count = width // 4
    per = 128 // (REACH * slots)
    own_live = table[2, k].astype(F32)
    row_live = table[3, k].astype(F32)
    col_live = table[4, k].astype(F32)
    corner_live = table[5, k].astype(F32)

    pad = jnp.zeros((2, chans, 128 + width), BF16)
    raw[0:2] = pad
    raw[rows + 5 : rows + 7] = pad
    raw[rows + 6 : rows + 8] = pad
    raw[2:5, :, 128:] = halo_ref[pl.ds(REACH * k, REACH)]
    raw[5 : 5 + rows, :, 128:] = slab_ref[0]
    lane = lax.broadcasted_iota(jnp.int32, (chans, 128), 1)
    for at in range(rows + REACH):
        low = (at % per) * REACH * slots + REACH * k
        inside = (lane >= low) & (lane < low + REACH)
        tile = halo_ref[REACH * slots + at // per].astype(F32)
        raw[2 + at, :, :128] = jnp.where(inside, tile, 0.0).astype(BF16)

    across = (((1,), (1,)), ((), ()))
    whole = (rows // WINDOW + 1) * WINDOW
    even = lax.dot_general(
        picks_ref[...],
        raw[0:whole].reshape(whole * chans, 128 + width),
        across,
        preferred_element_type=F32,
    ).astype(BF16)
    odd = lax.dot_general(
        picks_ref[...],
        raw[4 : 4 + rows].reshape(rows * chans, 128 + width),
        across,
        preferred_element_type=F32,
    ).astype(BF16)
    span = WINDOW * chans
    kinds = 3 * count
    row_at = lax.broadcasted_iota(jnp.int32, (kinds, 1), 0)
    for n in range(blocks + 1):
        source = even if n % 2 == 0 else odd
        lo = (n // 2) * span
        patch = jnp.concatenate(
            [source[b * kinds : (b + 1) * kinds, lo : lo + span] for b in range(3)], axis=1
        )
        got = silu(jnp.dot(patch, first_ref[...], preferred_element_type=F32))
        if n == 0:
            keep = jnp.where(row_at == 0, corner_live, row_live)
        else:
            keep = jnp.where(row_at == 0, col_live, 1.0)
        maps[n] = (got * keep).astype(BF16)

    mid = second_ref.shape[1] // 3
    total = None
    for b in range(3):
        upper = maps[0:blocks, b * count : (b + 1) * count, mid:].reshape(blocks * count, mid)
        lower = maps[1 : blocks + 1, b * count : (b + 1) * count, :].reshape(
            blocks * count, 2 * mid
        )
        term = jnp.dot(upper, second_ref[b, :mid], preferred_element_type=F32)
        term += jnp.dot(lower, second_ref[b, mid:], preferred_element_type=F32)
        total = term if total is None else total + term
    second = (silu(total) * own_live).astype(BF16)
    pre_act = jnp.dot(second, mix_ref[...], preferred_element_type=F32)
    out = (second.astype(F32) + silu(pre_act)).astype(BF16)
    out_ref[0] = out.reshape(blocks, count, out.shape[-1])


def body(state_tiles, water_mask, owner_tiles, neighbors, first_kernel, second_kernel, mix_kernel):
    owners = lax.axis_size("space")
    owner_index = lax.axis_index("space")
    groups = lax.axis_size(("chan", "sub"))
    group = lax.axis_index(("chan", "sub"))
    held, chans, rows, width = state_tiles.shape
    slots = owner_tiles.shape[1]
    tiles = water_mask.shape[0]
    lanes = (held + owners - 1) // owners
    per = 128 // (REACH * slots)
    col_tiles = (rows + REACH + per - 1) // per

    last_rows = lax.ppermute(
        state_tiles[:, :, rows - REACH :, :],
        ("chan", "sub"),
        [(i, (i + 1) % groups) for i in range(groups)],
    )

    tile_ids = jnp.arange(tiles, dtype=jnp.int32)
    local_ids = owner_index * held + jnp.arange(held, dtype=jnp.int32)
    local_water = lax.dynamic_slice_in_dim(water_mask, owner_index * held, held)
    wanted = jnp.concatenate([neighbors, tile_ids[:, None]], axis=1)
    held_as = ((wanted[:, :, None] == local_ids) & (local_water > 0)).astype(BF16)
    stands = (owner_tiles.reshape(-1)[:, None] == tile_ids[None, :]).astype(BF16)
    sel = exact("pt,tdj->pdj", stands, held_as).reshape(owners, slots, 4, held)
    first_group = group == 0
    sel_row = jnp.where(first_group, sel[:, :, 0], sel[:, :, 3])
    sel_col = sel[:, :, 1]
    sel_corner = jnp.where(first_group, sel[:, :, 2], sel[:, :, 1])
    from_here = jnp.sum(sel[:, :, 3].astype(F32), axis=2)
    order = jnp.cumsum(from_here, axis=1) - 1
    lane_ids = jnp.arange(lanes, dtype=F32)
    in_lane = (order[:, :, None] == lane_ids).astype(BF16)
    choose = exact("okq,okj->oqj", in_lane, sel[:, :, 3])

    slabs = exact("oqj,jcrw->oqrcw", choose, state_tiles).reshape(
        owners, lanes * rows, chans, width
    )
    row_part = exact("okj,jcyw->okycw", sel_row, last_rows).reshape(
        owners, slots * REACH, chans, width
    )
    col_own = exact("okj,jcyb->oyckb", sel_col, state_tiles[:, :, :, width - REACH :])
    col_corner = exact("okj,jcyb->oyckb", sel_corner, last_rows[:, :, :, width - REACH :])
    cols = jnp.concatenate([col_corner, col_own], axis=1)
    cols = jnp.pad(
        cols.reshape(owners, rows + REACH, chans, slots * REACH),
        ((0, 0), (0, col_tiles * per - rows - REACH), (0, 0), (0, 0)),
    )
    cols = cols.reshape(owners, col_tiles, per, chans, slots * REACH)
    cols = jnp.transpose(cols, (0, 1, 3, 2, 4)).reshape(
        owners, col_tiles, chans, per * slots * REACH
    )
    cols = jnp.pad(cols, ((0, 0), (0, 0), (0, 0), (0, width - per * slots * REACH)))
    outgoing = jnp.concatenate([slabs, row_part, cols], axis=1)
    incoming = lax.all_to_all(outgoing, "space", split_axis=0, concat_axis=0, tiled=True)
    halo = jnp.sum(incoming[:, lanes * rows :].astype(F32), axis=0).astype(BF16)

    my_tiles = lax.dynamic_slice_in_dim(owner_tiles, owner_index, 1, 0)[0]
    mine = my_tiles[:, None] == tile_ids[None, :]
    alive = jnp.sum(
        jnp.where(wanted[:, :, None] == tile_ids, water_mask, 0), axis=2
    )
    my_alive = jnp.sum(jnp.where(mine[:, :, None], alive[None], 0), axis=1)
    my_live = my_alive[:, 3]
    source = my_tiles // held
    ids = jnp.arange(slots, dtype=jnp.int32)
    earlier = (
        (source[:, None] == source[None, :]) & (my_live[None, :] > 0) & (ids[None, :] < ids[:, None])
    )
    lane_of = jnp.minimum(jnp.sum(earlier.astype(jnp.int32), axis=1), lanes - 1)
    table = jnp.stack(
        [
            source,
            lane_of,
            my_live,
            jnp.where(first_group, my_alive[:, 0], 1),
            my_alive[:, 1],
            jnp.where(first_group, my_alive[:, 2], my_alive[:, 1]),
        ]
    ).astype(jnp.int32)

    full_mix = lax.all_gather(mix_kernel, ("chan", "sub"), axis=1, tiled=True)
    mid, deep = second_kernel.shape[2:]
    by_col = jnp.transpose(first_kernel, (1, 0, 2, 3))
    spare = WINDOW - 3
    first_weights = jnp.stack(
        [
            jnp.pad(by_col, ((0, 0), (0, spare), (0, 0), (0, 0))),
            jnp.pad(by_col, ((0, 0), (2, spare - 2), (0, 0), (0, 0))),
        ],
        axis=3,
    ).reshape(3 * WINDOW * chans, 2 * mid)
    second_weights = jnp.transpose(second_kernel, (1, 0, 2, 3)).reshape(3, 3 * mid, deep)
    picks = jnp.asarray(column_picker(width, slots), BF16)

    blocks, count = rows // 4, width // 4
    fixed = lambda *dims: pl.BlockSpec(dims, lambda k, t: (0,) * len(dims))
    return pl.pallas_call(
        functools.partial(tile_kernel, slots),
        grid_spec=pltpu.PrefetchScalarGridSpec(
            num_scalar_prefetch=1,
            grid=(slots,),
            in_specs=[
                pl.BlockSpec((1, rows, chans, width), lambda k, t: (t[0, k], t[1, k], 0, 0)),
                fixed(*halo.shape),
                fixed(*picks.shape),
                fixed(*first_weights.shape),
                fixed(*second_weights.shape),
                fixed(*full_mix.shape),
            ],
            out_specs=pl.BlockSpec((1, blocks, count, deep), lambda k, t: (k, 0, 0, 0)),
            scratch_shapes=[
                pltpu.VMEM((rows + WINDOW, chans, 128 + width), BF16),
                pltpu.VMEM((blocks + 1, 3 * count, 2 * mid), BF16),
            ],
        ),
        out_shape=jax.ShapeDtypeStruct((slots, blocks, count, deep), BF16),
        compiler_params=pltpu.CompilerParams(vmem_limit_bytes=48 * 1024 * 1024),
        cost_estimate=pl.CostEstimate(
            flops=8 * 10**9, bytes_accessed=10 * 10**6, transcendentals=10 * 10**6
        ),
    )(table, incoming, halo, picks, first_weights, second_weights, full_mix)


def solution(mesh):
    placed = (
        P(("ens", "space"), None, ("chan", "sub"), None),
        P(),
        P(),
        P(),
        P(),
        P(),
        P(None, ("chan", "sub")),
    )
    return jax.shard_map(
        body,
        mesh=mesh,
        in_specs=placed,
        out_specs=P(("ens", "space"), ("chan", "sub"), None, None),
        check_vma=False,
    )
```

profile of v0, /device:TPU:0, one launch (start us, length us, event | category | flops | bytes accessed | tf_op | source)
XLA Modules:
  0.0 111.6 jit_solution(8987323984059511972)
XLA Ops:
  0.0 1.3 %slice.54 = bf16[16,16,3,128]{3,2,1,0:T(4,128)(2,1)S(1)} slice(bf16[16,16,32,128]{3,2,1,0:T(8,128)(2,1)} %param.8), slice={[0:16], [0:16], [29:32], [0:128]} | slice | bytes 393216 | tf_op jit(solution)/shard_map/slice | solution.py:136
  1.4 0.2 copy.59
  1.5 0.5 collective-permute-start
  2.0 3.6 %slice.50 = bf16[16,16,32,3]{3,2,1,0:T(8,128)(2,1)} slice(bf16[16,16,32,128]{3,2,1,0:T(8,128)(2,1)} %param.8), slice={[0:16], [0:16], [0:32], [125:128]} | slice | bytes 98304 | tf_op jit(solution)/shard_map/slice | solution.py:164
  5.6 0.0 copy-done.7
  5.6 0.1 eq.100
  5.7 0.0 copy-done.9
  5.7 0.1 dynamic-slice_compare_fusion
  5.8 0.0 copy-done.8
  5.8 0.1 compare_and_fusion
  5.9 0.2 fusion.13
  6.1 0.1 copy.36
  6.2 0.1 convert_reduce_fusion
  6.3 0.2 reduce_window_sum.11
  6.5 0.0 copy-done.2
  6.5 3.2 %convert_bitcast_fusion = bf16[4,4,32,16,128]{4,1,2,3,0:T(4,128)(2,1)} fusion(bf16[4,8,4,16]{3,1,0,2:T(8,128)(2,1)S(1)} %bitcast.119, f32[4,8]{1,0:T(4,128)S(1)} %broadcast_add_fusion, bf16[16,16,32,128]{3,2,1,0:T(8,128)(2,1)S(1)} %copy-done.2), kind=kOutput, calls=%fused_computation.5 | convolution fusion | flops 34607488 | bytes 4204544 | tf_op jit(solution)/shard_map/oqj,jcrw->oqrcw/dot_general | solution.py:18
  9.6 4.4 %copy.38 = bf16[4,4,32,16,128]{4,3,2,1,0:T(8,128)(2,1)} copy(bf16[4,4,32,16,128]{4,1,2,3,0:T(4,128)(2,1)} %convert_bitcast_fusion) | data formatting | bytes 4194304 | tf_op jit(solution)/shard_map/convert_element_type | solution.py:18
  14.0 0.0 copy-done.3
  14.0 1.9 %copy.53 = bf16[16,16,32,3]{2,0,3,1:T(8,128)(2,1)S(1)} copy(bf16[16,16,32,3]{3,2,1,0:T(8,128)(2,1)S(1)} %copy-done.3) | data formatting | bytes 98304
  16.0 0.2 fusion.7
  16.2 0.0 collective-permute-done
  16.2 0.1 slice.57
  16.3 0.4 copy.41
  16.8 0.1 fusion.8
  16.9 0.2 fusion.6
  17.1 0.1 copy.40
  17.2 0.7 copy.43
  17.9 1.0 pad_maximum_fusion
  18.8 3.4 %copy.44 = bf16[4,35,16,8,3]{2,0,4,3,1:T(4,128)(2,1)S(1)} copy(bf16[4,35,16,8,3]{1,3,4,2,0:T(8,128)(2,1)} %pad_maximum_fusion) | data formatting | bytes 215040 | tf_op jit(solution)/shard_map/concatenate | solution.py:166
  22.2 1.3 %copy.52 = bf16[4,7,16,120]{3,2,1,0:T(8,128)(2,1)S(1)} copy(bf16[4,7,16,120]{2,0,3,1:T(4,128)(2,1)S(1)} %bitcast.114) | data formatting | bytes 215040 | tf_op jit(solution)/shard_map/reshape | solution.py:172
  23.5 0.0 copy-done.4
  23.6 1.8 %fusion.1 = bf16[4,159,16,128]{3,2,1,0:T(8,128)(2,1)} fusion(bf16[4,7,16,120]{3,2,1,0:T(8,128)(2,1)S(1)} %copy.52, bf16[4,24,16,128]{3,2,1,0:T(8,128)(2,1)S(1)} %bitcast.116, bf16[4,128,16,128]{3,2,1,0:T(8,128)(2,1)S(1)} %bitcast.113), kind=kLoop, calls=%fused_computation.2 | loop fusion | flops 10420224 | bytes 5202944 | tf_op jit(solution)/shard_map/concatenate | solution.py:176
  25.3 6.0 %all-to-all-start = ((bf16[4,159,16,128]{3,2,1,0:T(8,128)(2,1)}), bf16[4,159,16,128]{3,2,1,0:T(8,128)(2,1)S(1)}, u32[]{:S(2)}, u32[]{:S(2)}) async-start(bf16[4,159,16,128]{3,2,1,0:T(8,128)(2,1)} %fusion.1), calls=%async_computation | async-start | bytes 5210112 | tf_op jit(solution)/shard_map/all_to_all | solution.py:177
  31.3 0.0 copy-done.6
  31.4 0.4 copy.46
  31.8 0.1 copy.54
  31.9 1.1 copy-done.5
  33.0 1.6 %copy.47 = bf16[3,3,256,512]{3,2,1,0:T(8,128)(2,1)} copy(bf16[3,3,256,512]{3,2,0,1:T(8,128)(2,1)S(1)} %bitcast.115) | data formatting | bytes 4718592 | tf_op jit(solution)/shard_map/transpose | solution.py:215
  34.6 0.2 select_reduce_fusion
  34.8 0.1 iota_compare_fusion.8
  34.9 0.2 select_reduce_fusion.1
  35.1 0.2 convert_reduce_fusion.1
  35.3 8.1 %all_gather.3.mix_ref = bf16[512,512]{1,0:T(8,128)(2,1)S(1)} all-gather(bf16[512,128]{1,0:T(8,128)(2,1)} %param.14), channel_id=1, replica_groups=mesh['ens'=2,'space'=4,'chan'=2,'sub'=2] {'chan','sub'}, dimensions={1}, use_global_device_ids=true | all-gather | bytes 655360 | tf_op jit(solution)/shard_map/all_gather | solution.py:204
  43.4 48.1 %all-to-all-done.slab_ref = bf16[4,159,16,128]{3,2,1,0:T(8,128)(2,1)S(1)} async-done(((bf16[4,159,16,128]{3,2,1,0:T(8,128)(2,1)}), bf16[4,159,16,128]{3,2,1,0:T(8,128)(2,1)S(1)}, u32[]{:S(2)}, u32[]{:S(2)}) %all-to-all-start) | async-done | bytes 2605088 | tf_op jit(solution)/shard_map/all_to_all | solution.py:177
  91.5 0.1 slice_reduce_fusion.halo_ref
  91.6 1.7 %copy-done = bf16[3,3,256,512]{3,2,1,0:T(8,128)(2,1)S(1)} copy-done((bf16[3,3,256,512]{3,2,1,0:T(8,128)(2,1)S(1)}, bf16[3,3,256,512]{3,2,1,0:T(8,128)(2,1)}, u32[]{:S(2)}) %copy-start) | copy-done | bytes 2359320
  93.2 0.9 copy-done.1
  94.1 17.4 %shard_map.82 = bf16[8,8,32,512]{3,2,1,0:T(8,128)(2,1)} custom-call(s32[6,8]{1,0:T(8,128)S(1)} %stack.16.table, bf16[4,159,16,128]{3,2,1,0:T(8,128)(2,1)S(1)} %all-to-all-done.slab_ref, bf16[31,16,128]{2,1,0:T(8,128)(2,1)S(1)} %slice_reduce_fusion.halo_ref, bf16[288,256]{1,0:T(8,128)(2,1)S(1)} %copy-done.1, bf16[384,512]{1,0:T(8,128)(2,1)S(1)} %bitcast.112, ...), custom_call_target="tpu_custom_call" | custom-call | flops 8000000000 | bytes 10000000 | tf_op jit(solution)/shard_map/pallas_call | solution.py:220
  (23 shorter events, 0.2 us)
Async XLA Ops:
  0.0 6.5 %copy-start.2 = (bf16[16,16,32,128]{3,2,1,0:T(8,128)(2,1)S(1)}, bf16[16,16,32,128]{3,2,1,0:T(8,128)(2,1)}, u32[]{:S(2)}) copy-start(bf16[16,16,32,128]{3,2,1,0:T(8,128)(2,1)} %param.8) | copy-start | bytes 6291460
  0.0 5.6 %copy-start.7 = (s32[4,8]{1,0:T(4,128)S(1)}, s32[4,8]{1,0:T(4,128)}, u32[]{:S(2)}) copy-start(s32[4,8]{1,0:T(4,128)} %param.10) | copy-start | bytes 388
  0.0 5.7 %copy-start.9 = (s32[64]{0:T(128)S(1)}, s32[64]{0:T(128)}, u32[]{:S(2)}) copy-start(s32[64]{0:T(128)} %param.9) | copy-start | bytes 772
  0.0 5.8 %copy-start.8 = (s32[64,3]{0,1:T(4,128)S(1)}, s32[64,3]{0,1:T(4,128)}, u32[]{:S(2)}) copy-start(s32[64,3]{0,1:T(4,128)} %param.11) | copy-start | bytes 2308
  1.5 14.7 %collective-permute-start = (bf16[16,16,3,128]{3,0,2,1:T(8,128)(2,1)S(1)}, bf16[16,16,3,128]{3,0,2,1:T(8,128)(2,1)S(1)}, u32[]{:S(2)}, u32[]{:S(2)}) collective-permute-start(bf16[16,16,3,128]{3,0,2,1:T(8,128)(2,1)S(1)} %copy.59), channel_id=1, source_target_pairs={{0,1},{1,2},{2,3},{3,0},{4,5},{5,6},{6,7},{7,4},{8,9},{9,10},{10,1... | collective-permute-start | bytes 589832 | tf_op jit(solution)/shard_map/ppermute | solution.py:135
  9.6 4.4 %copy-start.3 = (bf16[16,16,32,3]{3,2,1,0:T(8,128)(2,1)S(1)}, bf16[16,16,32,3]{3,2,1,0:T(8,128)(2,1)}, u32[]{:S(2)}) copy-start(bf16[16,16,32,3]{3,2,1,0:T(8,128)(2,1)} %slice.50) | copy-start | bytes 147460
  16.9 6.6 %copy-start.4 = (bf16[4,4,32,16,128]{4,3,2,1,0:T(8,128)(2,1)S(1)}, bf16[4,4,32,16,128]{4,3,2,1,0:T(8,128)(2,1)}, u32[]{:S(2)}) copy-start(bf16[4,4,32,16,128]{4,3,2,1,0:T(8,128)(2,1)} %copy.38) | copy-start | bytes 6291460
  25.3 6.0 %copy-start.6 = (bf16[3,3,16,256]{3,2,1,0:T(8,128)(2,1)S(1)}, bf16[3,3,16,256]{3,2,1,0:T(8,128)(2,1)}, u32[]{:S(2)}) copy-start(bf16[3,3,16,256]{3,2,1,0:T(8,128)(2,1)} %param.12) | copy-start | bytes 221188
  25.3 66.2 %all-to-all-start = ((bf16[4,159,16,128]{3,2,1,0:T(8,128)(2,1)}), bf16[4,159,16,128]{3,2,1,0:T(8,128)(2,1)S(1)}, u32[]{:S(2)}, u32[]{:S(2)}) async-start(bf16[4,159,16,128]{3,2,1,0:T(8,128)(2,1)} %fusion.1), calls=%async_computation | async-start | bytes 5210112 | tf_op jit(solution)/shard_map/all_to_all | solution.py:177
  31.3 1.7 %copy-start.5 = (bf16[3,3,256,512]{3,2,1,0:T(8,128)(2,1)S(1)}, bf16[3,3,256,512]{3,2,1,0:T(8,128)(2,1)}, u32[]{:S(2)}) copy-start(bf16[3,3,256,512]{3,2,1,0:T(8,128)(2,1)} %param.13) | copy-start | bytes 7077892
  91.6 1.7 %copy-start = (bf16[3,3,256,512]{3,2,1,0:T(8,128)(2,1)S(1)}, bf16[3,3,256,512]{3,2,1,0:T(8,128)(2,1)}, u32[]{:S(2)}) copy-start(bf16[3,3,256,512]{3,2,1,0:T(8,128)(2,1)} %copy.47) | copy-start | bytes 7077892
  93.2 0.9 copy-start.1
where the time goes:
time: 112 us
  waiting for transfers between devices  48.1 us (43%)
  local copies, waits for them, and re-layouts  23.3 us (21%)
  Pallas kernels  17.4 us (16%)
  blocking collectives  8.08 us (7%)
  starting transfers between devices  6.53 us (6%)
  other arithmetic  3.97 us (4%)
  matrix products  3.96 us (4%)
    all_to_all x1, waiting for transfers between devices, body(): lax.all_to_all(outgoing, 'space', split_axis=0, concat_axis=0, tiled=True)  48.1 us
    pallas_call x1, Pallas kernels, body(): pl.pallas_call(functools.partial(tile_kernel, slots), grid_spec=pltpu.Pre...  17.4 us
    all_gather x1, blocking collectives, body(): full_mix = lax.all_gather(mix_kernel, ('chan', 'sub'), axis=1, tiled=True)  8.08 us
    all_to_all x1, starting transfers between devices, body(): lax.all_to_all(outgoing, 'space', split_axis=0, concat_axis=0, tiled=True)  6.02 us
    unnamed x23, local copies, waits for them, and re-layouts  5.87 us
    convert_element_type x4, local copies, waits for them, and re-layouts, exact(): jnp.einsum(spec, one_hot, values, preferred_element_type=F32).astype(BF16)  5.21 us
    dot_general x4, matrix products, exact(): jnp.einsum(spec, one_hot, values, preferred_element_type=F32).astype(BF16)  3.77 us
    slice x1, local copies, waits for them, and re-layouts, body(): state_tiles[:, :, :, width - REACH:]  3.56 us
  transfers between devices with their start and end apart: 2, of which 1 were waited for; matrix products, arithmetic and copies ran while one was open for 15% of the time, Pallas kernels for 0%

commit v1 on v0

--- a/solution.py
+++ b/solution.py
@@ -38,21 +38,11 @@
     return x * (1.0 / (1.0 + jnp.exp(-x)))
 
 
-def tile_kernel(
-    slots,
-    table,
-    slab_ref,
-    halo_ref,
-    picks_ref,
-    first_ref,
-    second_ref,
-    mix_ref,
-    out_ref,
-    raw,
-    maps,
-):
+def tile_kernel(slots, table, *refs):
+    slab_refs = refs[:-8]
+    halo_ref, picks_ref, first_ref, second_ref, mix_ref, out_ref, raw, maps = refs[-8:]
     k = pl.program_id(0)
-    rows, chans, width = slab_ref.shape[1:]
+    rows, chans, width = slab_refs[0].shape[1:]
     blocks = rows // 4
     count = width // 4
     per = 128 // (REACH * slots)
@@ -66,7 +56,12 @@
     raw[rows + 5 : rows + 7] = pad
     raw[rows + 6 : rows + 8] = pad
     raw[2:5, :, 128:] = halo_ref[pl.ds(REACH * k, REACH)]
-    raw[5 : 5 + rows, :, 128:] = slab_ref[0]
+    for shift, slab_ref in enumerate(slab_refs):
+
+        @pl.when(table[0, k] == shift)
+        def _(slab_ref=slab_ref):
+            raw[5 : 5 + rows, :, 128:] = slab_ref[0]
+
     lane = lax.broadcasted_iota(jnp.int32, (chans, 128), 1)
     for at in range(rows + REACH):
         low = (at % per) * REACH * slots + REACH * k
@@ -143,7 +138,10 @@
     local_water = lax.dynamic_slice_in_dim(water_mask, owner_index * held, held)
     wanted = jnp.concatenate([neighbors, tile_ids[:, None]], axis=1)
     held_as = ((wanted[:, :, None] == local_ids) & (local_water > 0)).astype(BF16)
-    stands = (owner_tiles.reshape(-1)[:, None] == tile_ids[None, :]).astype(BF16)
+    turned = lax.dynamic_slice_in_dim(
+        jnp.concatenate([owner_tiles, owner_tiles], axis=0), owner_index, owners, 0
+    )
+    stands = (turned.reshape(-1)[:, None] == tile_ids[None, :]).astype(BF16)
     sel = exact("pt,tdj->pdj", stands, held_as).reshape(owners, slots, 4, held)
     first_group = group == 0
     sel_row = jnp.where(first_group, sel[:, :, 0], sel[:, :, 3])
@@ -155,9 +153,16 @@
     in_lane = (order[:, :, None] == lane_ids).astype(BF16)
     choose = exact("okq,okj->oqj", in_lane, sel[:, :, 3])
 
-    slabs = exact("oqj,jcrw->oqrcw", choose, state_tiles).reshape(
-        owners, lanes * rows, chans, width
-    )
+    def send(shift, x):
+        if shift == 0:
+            return x
+        return lax.ppermute(x, "space", [(i, (i + shift) % owners) for i in range(owners)])
+
+    slabs = [None] * owners
+    for shift in list(range(1, owners)) + [0]:
+        slab = exact("qj,jcrw->qrcw", choose[shift], state_tiles)
+        slabs[shift] = send(shift, slab)
+
     row_part = exact("okj,jcyw->okycw", sel_row, last_rows).reshape(
         owners, slots * REACH, chans, width
     )
@@ -173,11 +178,10 @@
         owners, col_tiles, chans, per * slots * REACH
     )
     cols = jnp.pad(cols, ((0, 0), (0, 0), (0, 0), (0, width - per * slots * REACH)))
-    outgoing = jnp.concatenate([slabs, row_part, cols], axis=1)
-    incoming = lax.all_to_all(outgoing, "space", split_axis=0, concat_axis=0, tiled=True)
-    halo = jnp.sum(incoming[:, lanes * rows :].astype(F32), axis=0).astype(BF16)
-
-    my_tiles = lax.dynamic_slice_in_dim(owner_tiles, owner_index, 1, 0)[0]
+    outgoing = jnp.concatenate([row_part, cols], axis=1)
+    halo = sum(send(shift, outgoing[shift]).astype(F32) for shift in range(owners)).astype(BF16)
+
+    my_tiles = turned[0]
     mine = my_tiles[:, None] == tile_ids[None, :]
     alive = jnp.sum(
         jnp.where(wanted[:, :, None] == tile_ids, water_mask, 0), axis=2
@@ -192,7 +196,7 @@
     lane_of = jnp.minimum(jnp.sum(earlier.astype(jnp.int32), axis=1), lanes - 1)
     table = jnp.stack(
         [
-            source,
+            (owner_index - source + owners) % owners,
             lane_of,
             my_live,
             jnp.where(first_group, my_alive[:, 0], 1),
@@ -223,7 +227,13 @@
             num_scalar_prefetch=1,
             grid=(slots,),
             in_specs=[
-                pl.BlockSpec((1, rows, chans, width), lambda k, t: (t[0, k], t[1, k], 0, 0)),
+                *[
+                    pl.BlockSpec(
+                        (1, rows, chans, width),
+                        lambda k, t, d=d: (jnp.where(t[0, k] == d, t[1, k], 0), 0, 0, 0),
+                    )
+                    for d in range(owners)
+                ],
                 fixed(*halo.shape),
                 fixed(*picks.shape),
                 fixed(*first_weights.shape),
@@ -241,7 +251,7 @@
         cost_estimate=pl.CostEstimate(
             flops=8 * 10**9, bytes_accessed=10 * 10**6, transcendentals=10 * 10**6
         ),
-    )(table, incoming, halo, picks, first_weights, second_weights, full_mix)
+    )(table, *slabs, halo, picks, first_weights, second_weights, full_mix)
 
 
 def solution(mesh):

time: 112 us -> 94.2 us (0.84)
  waiting for transfers between devices: 48.1 us -> 8.97 us
  starting transfers between devices: 6.53 us -> 26.1 us
  local copies, waits for them, and re-layouts: 23.3 us -> 17.7 us
  matrix products: 3.96 us -> 7.78 us
  other arithmetic: 3.97 us -> 6.73 us
  Pallas kernels: 17.4 us -> 18.9 us
    all_to_all x1 -> x0, waiting for transfers between devices: 48.1 us -> none  [body(): lax.all_to_all(outgoing, 'space', split_axis=0, concat_axis=0, tiled=True)]
    ppermute x0 -> x6, starting transfers between devices: none -> 25.6 us  [send(): lax.ppermute(x, 'space', [(i, (i + shift) % owners) for i in range(owners)])]
    ppermute x0 -> x6, waiting for transfers between devices: none -> 8.97 us  [send(): lax.ppermute(x, 'space', [(i, (i + shift) % owners) for i in range(owners)])]
    all_to_all x1 -> x0, starting transfers between devices: 6.02 us -> none  [body(): lax.all_to_all(outgoing, 'space', split_axis=0, concat_axis=0, tiled=True)]
    convert_element_type x4 -> x3, local copies, waits for them, and re-layouts: 5.21 us -> 0.82 us  [exact(): jnp.einsum(spec, one_hot, values, preferred_element_type=F32).astype(BF16)]
    dot_general x4 -> x8, matrix products: 3.77 us -> 7.59 us  [exact(): jnp.einsum(spec, one_hot, values, preferred_element_type=F32).astype(BF16)]
    dot_general x0 -> x4, local copies, waits for them, and re-layouts: none -> 3.75 us  [exact(): jnp.einsum(spec, one_hot, values, preferred_element_type=F32).astype(BF16)]
    unnamed x23 -> x15, local copies, waits for them, and re-layouts: 5.87 us -> 3.34 us
  transfers between devices with their start and end apart: 2 -> 7, of which waited for: 1 -> 1; matrix products, arithmetic and copies ran while one was open for 15% -> 33% of each run, Pallas kernels for 0% -> 0%
where the time goes in v1:
time: 94.2 us; the launch traced here: 93.8 us
  starting transfers between devices  26.1 us (28%)
  Pallas kernels  18.9 us (20%)
  local copies, waits for them, and re-layouts  17.7 us (19%)
  waiting for transfers between devices  8.97 us (10%)
  matrix products  7.78 us (8%)
  blocking collectives  7.43 us (8%)
  other arithmetic  6.73 us (7%)
    ppermute x6, starting transfers between devices, send(): lax.ppermute(x, 'space', [(i, (i + shift) % owners) for i in range(owners)])  25.6 us
    pallas_call x1, Pallas kernels, body(): pl.pallas_call(functools.partial(tile_kernel, slots), grid_spec=pltpu.Pre...  18.9 us
    ppermute x6, waiting for transfers between devices, send(): lax.ppermute(x, 'space', [(i, (i + shift) % owners) for i in range(owners)])  8.97 us
    dot_general x8, matrix products, exact(): jnp.einsum(spec, one_hot, values, preferred_element_type=F32).astype(BF16)  7.59 us
    all_gather x1, blocking collectives, body(): full_mix = lax.all_gather(mix_kernel, ('chan', 'sub'), axis=1, tiled=True)  7.43 us
    dot_general x4, local copies, waits for them, and re-layouts, exact(): jnp.einsum(spec, one_hot, values, preferred_element_type=F32).astype(BF16)  3.75 us
    unnamed x15, local copies, waits for them, and re-layouts  3.34 us
    concatenate x1, local copies, waits for them, and re-layouts, body(): cols = jnp.concatenate([col_corner, col_own], axis=1)  2.6 us
  transfers between devices with their start and end apart: 7, of which 1 were waited for; matrix products, arithmetic and copies ran while one was open for 33% of the time, Pallas kernels for 0%

profile of v1, /device:TPU:0, one launch (start us, length us, event | category | flops | bytes accessed | tf_op | source)
XLA Modules:
  0.0 93.8 jit_solution(13793995669225041927)
XLA Ops:
  0.0 1.2 %slice.90 = bf16[16,16,3,128]{3,2,1,0:T(4,128)(2,1)S(1)} slice(bf16[16,16,32,128]{3,2,1,0:T(8,128)(2,1)} %param.8), slice={[0:16], [0:16], [29:32], [0:128]} | slice | bytes 393216 | tf_op jit(solution)/shard_map/slice | solution.py:131
  1.2 0.2 copy.96
  1.4 0.5 collective-permute-start.3
  1.9 0.8 pad_add_fusion
  2.8 0.7 dynamic-slice_compare_fusion
  3.5 0.7 pad_add_fusion.1
  4.3 0.2 fusion.15
  4.7 0.2 reduce_window_sum.11
  4.8 0.1 convolution_convert_fusion.3
  5.0 2.9 %fusion.33 = bf16[4,16,32,128]{3,0,2,1:T(4,128)(2,1)S(1)} fusion(bf16[4,4,16]{2,1,0:T(4,128)(2,1)S(1)} %convolution_convert_fusion.3, bf16[16,16,32,128]{3,2,1,0:T(8,128)(2,1)} %param.8), kind=kOutput, calls=%fused_computation.79 | convolution fusion | flops 8388608 | bytes 2622464 | tf_op jit(solution)/shard_map/qj,jcrw->qrcw/dot_general | solution.py:18
  7.9 1.1 %copy.98 = bf16[4,16,32,128]{3,1,2,0:T(8,128)(2,1)} copy(bf16[4,16,32,128]{3,0,2,1:T(4,128)(2,1)S(1)} %fusion.33) | data formatting | bytes 1048576 | tf_op jit(solution)/shard_map/qj,jcrw->qrcw/dot_general | solution.py:18
  9.0 2.7 %collective-permute-start = (bf16[4,32,16,128]{3,2,1,0:T(8,128)(2,1)}, bf16[4,32,16,128]{3,2,1,0:T(8,128)(2,1)}, u32[]{:S(2)}, u32[]{:S(2)}) collective-permute-start(bf16[4,32,16,128]{3,2,1,0:T(8,128)(2,1)} %bitcast.145), channel_id=1, source_target_pairs={{0,4},{4,8},{8,12},{12,0},{1,5},{5,9},{9,13},{13,1},{2,6},{6,10},{... | collective-permute-start | bytes 1572872 | tf_op jit(solution)/shard_map/ppermute | solution.py:159
  11.7 1.3 %fusion.32 = bf16[4,16,32,128]{3,0,2,1:T(4,128)(2,1)S(1)} fusion(bf16[4,4,16]{2,1,0:T(4,128)(2,1)S(1)} %convolution_convert_fusion.3, bf16[16,16,32,128]{3,2,1,0:T(8,128)(2,1)S(1)} %copy-done.1), kind=kOutput, calls=%fused_computation.77 | convolution fusion | flops 8388608 | bytes 2622464 | tf_op jit(solution)/shard_map/qj,jcrw->qrcw/dot_general | solution.py:18
  13.0 1.1 %copy.99 = bf16[4,16,32,128]{3,1,2,0:T(8,128)(2,1)} copy(bf16[4,16,32,128]{3,0,2,1:T(4,128)(2,1)S(1)} %fusion.32) | data formatting | bytes 1048576 | tf_op jit(solution)/shard_map/qj,jcrw->qrcw/dot_general | solution.py:18
  14.1 2.6 %collective-permute-start.1 = (bf16[4,32,16,128]{3,2,1,0:T(8,128)(2,1)}, bf16[4,32,16,128]{3,2,1,0:T(8,128)(2,1)}, u32[]{:S(2)}, u32[]{:S(2)}) collective-permute-start(bf16[4,32,16,128]{3,2,1,0:T(8,128)(2,1)} %bitcast.146), channel_id=1, source_target_pairs={{0,8},{4,12},{8,0},{12,4},{1,9},{5,13},{9,1},{13,5},{2,10},{6,14},... | collective-permute-start | bytes 1572872 | tf_op jit(solution)/shard_map/ppermute | solution.py:159
  16.7 1.3 %fusion.31 = bf16[4,16,32,128]{3,0,2,1:T(4,128)(2,1)S(1)} fusion(bf16[4,4,16]{2,1,0:T(4,128)(2,1)S(1)} %convolution_convert_fusion.3, bf16[16,16,32,128]{3,2,1,0:T(8,128)(2,1)S(1)} %copy-done.1), kind=kOutput, calls=%fused_computation.75 | convolution fusion | flops 8388608 | bytes 2622464 | tf_op jit(solution)/shard_map/qj,jcrw->qrcw/dot_general | solution.py:18
  18.1 1.1 %copy.100 = bf16[4,16,32,128]{3,1,2,0:T(8,128)(2,1)} copy(bf16[4,16,32,128]{3,0,2,1:T(4,128)(2,1)S(1)} %fusion.31) | data formatting | bytes 1048576 | tf_op jit(solution)/shard_map/qj,jcrw->qrcw/dot_general | solution.py:18
  19.2 1.3 %collective-permute-start.2 = (bf16[4,32,16,128]{3,2,1,0:T(8,128)(2,1)}, bf16[4,32,16,128]{3,2,1,0:T(8,128)(2,1)}, u32[]{:S(2)}, u32[]{:S(2)}) collective-permute-start(bf16[4,32,16,128]{3,2,1,0:T(8,128)(2,1)} %bitcast.147), channel_id=1, source_target_pairs={{0,12},{4,0},{8,4},{12,8},{1,13},{5,1},{9,5},{13,9},{2,14},{6,2},{... | collective-permute-start | bytes 1572872 | tf_op jit(solution)/shard_map/ppermute | solution.py:159
  20.5 0.2 select_reduce_fusion
  20.8 0.5 and_select_fusion.1
  21.4 0.1 select_reduce_fusion.1
  21.6 0.5 broadcast_select_fusion
  22.1 0.6 slice_bitcast_fusion.17
  22.7 1.3 %fusion.34 = bf16[4,16,32,128]{3,0,2,1:T(4,128)(2,1)S(1)} fusion(bf16[4,4,16]{2,1,0:T(4,128)(2,1)S(1)} %convolution_convert_fusion.3, bf16[16,16,32,128]{3,2,1,0:T(8,128)(2,1)S(1)} %copy-done.1), kind=kOutput, calls=%fused_computation.81 | convolution fusion | flops 8388608 | bytes 2622464 | tf_op jit(solution)/shard_map/qj,jcrw->qrcw/dot_general | solution.py:18
  24.0 2.0 %slice.79 = bf16[16,16,32,3]{3,2,1,0:T(8,128)(2,1)} slice(bf16[16,16,32,128]{3,2,1,0:T(8,128)(2,1)S(1)} %copy-done.1), slice={[0:16], [0:16], [0:32], [125:128]} | slice | bytes 98304 | tf_op jit(solution)/shard_map/slice | solution.py:169
  26.0 3.0 %copy.74 = bf16[16,16,32,3]{2,0,3,1:T(8,128)(2,1)S(1)} copy(bf16[16,16,32,3]{3,2,1,0:T(8,128)(2,1)} %slice.79) | data formatting | bytes 98304
  29.0 0.2 fusion.1
  29.3 0.2 convert_reduce_fusion.1
  29.4 0.5 minimum_bitcast_fusion
  30.1 0.4 copy.59
  30.5 0.1 fusion.2
  30.7 0.2 fusion
  31.0 0.7 copy.61
  31.6 0.2 pad_maximum_fusion
  31.9 2.6 %copy.62 = bf16[4,35,16,8,3]{2,0,4,3,1:T(4,128)(2,1)S(1)} copy(bf16[4,35,16,8,3]{1,3,4,2,0:T(8,128)(2,1)S(1)} %pad_maximum_fusion) | data formatting | bytes 215040 | tf_op jit(solution)/shard_map/concatenate | solution.py:171
  34.5 1.3 %copy.73 = bf16[4,7,16,120]{3,2,1,0:T(8,128)(2,1)S(1)} copy(bf16[4,7,16,120]{2,0,3,1:T(4,128)(2,1)S(1)} %bitcast.151) | data formatting | bytes 215040 | tf_op jit(solution)/shard_map/reshape | solution.py:177
  35.9 0.8 slice_bitcast_fusion.2
  36.7 0.7 collective-permute-start.4
  37.5 0.4 copy.64
  37.9 0.3 copy.97
  38.4 0.2 copy.65
  38.5 0.7 stack.16.table
  39.2 3.2 %collective-permute-start.6 = (bf16[31,16,128]{2,1,0:T(8,128)(2,1)}, bf16[31,16,128]{2,1,0:T(8,128)(2,1)S(1)}, u32[]{:S(2)}, u32[]{:S(2)}) collective-permute-start(bf16[31,16,128]{2,1,0:T(8,128)(2,1)} %get-tuple-element.8), channel_id=1, source_target_pairs={{0,12},{4,0},{8,4},{12,8},{1,13},{5,1},{9,5},{13,9},{2,14},{6,2},{... | collective-permute-start | bytes 380936 | tf_op jit(solution)/shard_map/ppermute | solution.py:159
  42.4 9.0 %collective-permute-done.4 = bf16[31,16,128]{2,1,0:T(8,128)(2,1)S(1)} collective-permute-done((bf16[31,16,128]{2,1,0:T(8,128)(2,1)}, bf16[31,16,128]{2,1,0:T(8,128)(2,1)S(1)}, u32[]{:S(2)}, u32[]{:S(2)}) %collective-permute-start.4) | collective-permute-done | bytes 127008 | tf_op jit(solution)/shard_map/ppermute | solution.py:159
  51.3 15.1 %collective-permute-start.5 = (bf16[31,16,128]{2,1,0:T(8,128)(2,1)}, bf16[31,16,128]{2,1,0:T(8,128)(2,1)S(1)}, u32[]{:S(2)}, u32[]{:S(2)}) collective-permute-start(bf16[31,16,128]{2,1,0:T(8,128)(2,1)} %get-tuple-element.9), channel_id=1, source_target_pairs={{0,8},{4,12},{8,0},{12,4},{1,9},{5,13},{9,1},{13,5},{2,10},{6,14},... | collective-permute-start | bytes 380936 | tf_op jit(solution)/shard_map/ppermute | solution.py:159
  66.4 7.4 %all_gather.3.refs_8_ = bf16[512,512]{1,0:T(8,128)(2,1)S(1)} all-gather(bf16[512,128]{1,0:T(8,128)(2,1)} %param.14), channel_id=1, replica_groups=mesh['ens'=2,'space'=4,'chan'=2,'sub'=2] {'chan','sub'}, dimensions={1}, use_global_device_ids=true | all-gather | bytes 655360 | tf_op jit(solution)/shard_map/all_gather | solution.py:208
  73.9 1.0 %fusion.11.refs_4_ = bf16[31,16,128]{2,1,0:T(8,128)(2,1)S(1)} fusion(bf16[31,16,128]{2,1,0:T(8,128)(2,1)S(1)} %collective-permute-done.6, bf16[31,16,128]{2,1,0:T(8,128)(2,1)S(1)} %collective-permute-done.5, bf16[31,16,128]{2,1,0:T(8,128)(2,1)S(1)} %collective-permute-done.4, bf16[4,31,16,128]{3,2,1,0:T(8,128)(2,1)} %copy-done.3), kind=kLoop, calls=%fused_computation.23 | loop fusion | flops 507904 | bytes 634880 | tf_op jit(solution)/shard_map/convert_element_type | solution.py:182
  74.9 18.9 %shard_map.82 = bf16[8,8,32,512]{3,2,1,0:T(8,128)(2,1)} custom-call(s32[6,8]{1,0:T(8,128)S(1)} %stack.16.table, bf16[4,32,16,128]{3,2,1,0:T(8,128)(2,1)S(1)} %bitcast.149, bf16[4,32,16,128]{3,2,1,0:T(8,128)(2,1)} %collective-permute-done.refs_1_, bf16[4,32,16,128]{3,2,1,0:T(8,128)(2,1)} %collective-permute-done.1.refs_2_, ...), custom_call_target="tpu_custom_call" | custom-call | flops 8000000000 | bytes 10000000 | tf_op jit(solution)/shard_map/pallas_call | solution.py:224
  (36 shorter events, 1.0 us)
Async XLA Ops:
  1.2 10.5 %copy-start.1 = (bf16[16,16,32,128]{3,2,1,0:T(8,128)(2,1)S(1)}, bf16[16,16,32,128]{3,2,1,0:T(8,128)(2,1)}, u32[]{:S(2)}) copy-start(bf16[16,16,32,128]{3,2,1,0:T(8,128)(2,1)} %param.8) | copy-start | bytes 6291460
  1.4 28.6 %collective-permute-start.3 = (bf16[16,16,3,128]{3,0,2,1:T(8,128)(2,1)S(1)}, bf16[16,16,3,128]{3,0,2,1:T(8,128)(2,1)S(1)}, u32[]{:S(2)}, u32[]{:S(2)}) collective-permute-start(bf16[16,16,3,128]{3,0,2,1:T(8,128)(2,1)S(1)} %copy.96), channel_id=1, source_target_pairs={{0,1},{1,2},{2,3},{3,0},{4,5},{5,6},{6,7},{7,4},{8,9},{9,10},{10,1... | collective-permute-start | bytes 589832 | tf_op jit(solution)/shard_map/ppermute | solution.py:130
  9.0 65.9 %collective-permute-start = (bf16[4,32,16,128]{3,2,1,0:T(8,128)(2,1)}, bf16[4,32,16,128]{3,2,1,0:T(8,128)(2,1)}, u32[]{:S(2)}, u32[]{:S(2)}) collective-permute-start(bf16[4,32,16,128]{3,2,1,0:T(8,128)(2,1)} %bitcast.145), channel_id=1, source_target_pairs={{0,4},{4,8},{8,12},{12,0},{1,5},{5,9},{9,13},{13,1},{2,6},{6,10},{... | collective-permute-start | bytes 1572872 | tf_op jit(solution)/shard_map/ppermute | solution.py:159
  14.1 6.4 %copy-start.5 = (s32[64]{0:T(128)S(1)}, s32[64]{0:T(128)}, u32[]{:S(2)}) copy-start(s32[64]{0:T(128)} %param.9) | copy-start | bytes 772
  14.1 60.7 %collective-permute-start.1 = (bf16[4,32,16,128]{3,2,1,0:T(8,128)(2,1)}, bf16[4,32,16,128]{3,2,1,0:T(8,128)(2,1)}, u32[]{:S(2)}, u32[]{:S(2)}) collective-permute-start(bf16[4,32,16,128]{3,2,1,0:T(8,128)(2,1)} %bitcast.146), channel_id=1, source_target_pairs={{0,8},{4,12},{8,0},{12,4},{1,9},{5,13},{9,1},{13,5},{2,10},{6,14},... | collective-permute-start | bytes 1572872 | tf_op jit(solution)/shard_map/ppermute | solution.py:159
  19.2 55.7 %collective-permute-start.2 = (bf16[4,32,16,128]{3,2,1,0:T(8,128)(2,1)}, bf16[4,32,16,128]{3,2,1,0:T(8,128)(2,1)}, u32[]{:S(2)}, u32[]{:S(2)}) collective-permute-start(bf16[4,32,16,128]{3,2,1,0:T(8,128)(2,1)} %bitcast.147), channel_id=1, source_target_pairs={{0,12},{4,0},{8,4},{12,8},{1,13},{5,1},{9,5},{13,9},{2,14},{6,2},{... | collective-permute-start | bytes 1572872 | tf_op jit(solution)/shard_map/ppermute | solution.py:159
  31.9 5.5 %copy-start.4 = (bf16[3,3,16,256]{3,2,1,0:T(8,128)(2,1)S(1)}, bf16[3,3,16,256]{3,2,1,0:T(8,128)(2,1)}, u32[]{:S(2)}) copy-start(bf16[3,3,16,256]{3,2,1,0:T(8,128)(2,1)} %param.12) | copy-start | bytes 221188
  35.9 2.4 %copy-start.3 = (bf16[4,31,16,128]{3,2,1,0:T(8,128)(2,1)}, bf16[4,31,16,128]{3,2,1,0:T(8,128)(2,1)S(1)}, u32[]{:S(2)}) copy-start(bf16[4,31,16,128]{3,2,1,0:T(8,128)(2,1)S(1)} %fusion.8) | copy-start | bytes 1523716
  36.7 1.7 %copy-start.2 = (bf16[3,3,256,512]{3,2,1,0:T(8,128)(2,1)S(1)}, bf16[3,3,256,512]{3,2,1,0:T(8,128)(2,1)}, u32[]{:S(2)}) copy-start(bf16[3,3,256,512]{3,2,1,0:T(8,128)(2,1)} %param.13) | copy-start | bytes 7077892
  36.7 14.6 %collective-permute-start.4 = (bf16[31,16,128]{2,1,0:T(8,128)(2,1)}, bf16[31,16,128]{2,1,0:T(8,128)(2,1)S(1)}, u32[]{:S(2)}, u32[]{:S(2)}) collective-permute-start(bf16[31,16,128]{2,1,0:T(8,128)(2,1)} %get-tuple-element.7), channel_id=1, source_target_pairs={{0,4},{4,8},{8,12},{12,0},{1,5},{5,9},{9,13},{13,1},{2,6},{6,10},{... | collective-permute-start | bytes 380936 | tf_op jit(solution)/shard_map/ppermute | solution.py:159
  38.4 36.5 %copy-start = (bf16[288,256]{1,0:T(8,128)(2,1)S(1)}, bf16[288,256]{1,0:T(8,128)(2,1)}, u32[]{:S(2)}) copy-start(bf16[288,256]{1,0:T(8,128)(2,1)} %constant.65.clone.refs_5_) | copy-start | bytes 442372
  39.2 34.6 %collective-permute-start.6 = (bf16[31,16,128]{2,1,0:T(8,128)(2,1)}, bf16[31,16,128]{2,1,0:T(8,128)(2,1)S(1)}, u32[]{:S(2)}, u32[]{:S(2)}) collective-permute-start(bf16[31,16,128]{2,1,0:T(8,128)(2,1)} %get-tuple-element.8), channel_id=1, source_target_pairs={{0,12},{4,0},{8,4},{12,8},{1,13},{5,1},{9,5},{13,9},{2,14},{6,2},{... | collective-permute-start | bytes 380936 | tf_op jit(solution)/shard_map/ppermute | solution.py:159
  51.3 22.5 %collective-permute-start.5 = (bf16[31,16,128]{2,1,0:T(8,128)(2,1)}, bf16[31,16,128]{2,1,0:T(8,128)(2,1)S(1)}, u32[]{:S(2)}, u32[]{:S(2)}) collective-permute-start(bf16[31,16,128]{2,1,0:T(8,128)(2,1)} %get-tuple-element.9), channel_id=1, source_target_pairs={{0,8},{4,12},{8,0},{12,4},{1,9},{5,13},{9,1},{13,5},{2,10},{6,14},... | collective-permute-start | bytes 380936 | tf_op jit(solution)/shard_map/ppermute | solution.py:159

commit v2 on v1

--- a/solution.py
+++ b/solution.py
@@ -178,7 +178,9 @@
         owners, col_tiles, chans, per * slots * REACH
     )
     cols = jnp.pad(cols, ((0, 0), (0, 0), (0, 0), (0, width - per * slots * REACH)))
+    full_mix = lax.all_gather(mix_kernel, ("chan", "sub"), axis=1, tiled=True)
     outgoing = jnp.concatenate([row_part, cols], axis=1)
+    outgoing, full_mix = lax.optimization_barrier((outgoing, full_mix))
     halo = sum(send(shift, outgoing[shift]).astype(F32) for shift in range(owners)).astype(BF16)
 
     my_tiles = turned[0]
@@ -205,7 +207,6 @@
         ]
     ).astype(jnp.int32)
 
-    full_mix = lax.all_gather(mix_kernel, ("chan", "sub"), axis=1, tiled=True)
     mid, deep = second_kernel.shape[2:]
     by_col = jnp.transpose(first_kernel, (1, 0, 2, 3))
     spare = WINDOW - 3

time: 94.2 us -> 96 us (1.019)
  local copies, waits for them, and re-layouts: 17.7 us -> 20.7 us
  waiting for transfers between devices: 8.97 us -> 7.56 us
  starting transfers between devices: 26.1 us -> 25.1 us
    unnamed x15 -> x25, local copies, waits for them, and re-layouts: 3.34 us -> 6.44 us
    ppermute x6, waiting for transfers between devices: 8.97 us -> 7.55 us  [send(): lax.ppermute(x, 'space', [(i, (i + shift) % owners) for i in range(owners)])]
  transfers between devices with their start and end apart: 7 -> 7, of which waited for: 1 -> 2; matrix products, arithmetic and copies ran while one was open for 33% -> 34% of each run, Pallas kernels for 0% -> 0%
where the time goes in v2:
time: 96 us; the launch traced here: 95.6 us
  starting transfers between devices  25.1 us (26%)
  local copies, waits for them, and re-layouts  20.7 us (22%)
  Pallas kernels  19.3 us (20%)
  matrix products  7.78 us (8%)
  blocking collectives  7.6 us (8%)
  waiting for transfers between devices  7.56 us (8%)
  other arithmetic  7.35 us (8%)
    ppermute x6, starting transfers between devices, send(): lax.ppermute(x, 'space', [(i, (i + shift) % owners) for i in range(owners)])  24.6 us
    pallas_call x1, Pallas kernels, body(): pl.pallas_call(functools.partial(tile_kernel, slots), grid_spec=pltpu.Pre...  19.3 us
    all_gather x1, blocking collectives, body(): full_mix = lax.all_gather(mix_kernel, ('chan', 'sub'), axis=1, tiled=True)  7.6 us
    dot_general x8, matrix products, exact(): jnp.einsum(spec, one_hot, values, preferred_element_type=F32).astype(BF16)  7.59 us
    ppermute x6, waiting for transfers between devices, send(): lax.ppermute(x, 'space', [(i, (i + shift) % owners) for i in range(owners)])  7.55 us
    unnamed x25, local copies, waits for them, and re-layouts  6.44 us
    dot_general x4, local copies, waits for them, and re-layouts, exact(): jnp.einsum(spec, one_hot, values, preferred_element_type=F32).astype(BF16)  3.77 us
    concatenate x1, local copies, waits for them, and re-layouts, body(): cols = jnp.concatenate([col_corner, col_own], axis=1)  2.6 us
  transfers between devices with their start and end apart: 7, of which 2 were waited for; matrix products, arithmetic and copies ran while one was open for 34% of the time, Pallas kernels for 0%

profile of v2, /device:TPU:0, one launch (start us, length us, event | category | flops | bytes accessed | tf_op | source)
XLA Modules:
  0.0 95.6 jit_solution(16726609253038120644)
XLA Ops:
  0.0 1.2 %slice.90 = bf16[16,16,3,128]{3,2,1,0:T(4,128)(2,1)S(1)} slice(bf16[16,16,32,128]{3,2,1,0:T(8,128)(2,1)} %param.8), slice={[0:16], [0:16], [29:32], [0:128]} | slice | bytes 393216 | tf_op jit(solution)/shard_map/slice | solution.py:131
  1.4 0.5 collective-permute-start.3
  1.9 0.8 pad_add_fusion
  2.8 0.7 dynamic-slice_compare_fusion
  3.5 0.7 pad_add_fusion.1
  4.3 0.2 fusion.15
  4.7 0.2 reduce_window_sum.11
  5.0 2.9 %fusion.33 = bf16[4,16,32,128]{3,0,2,1:T(4,128)(2,1)S(1)} fusion(bf16[4,4,16]{2,1,0:T(4,128)(2,1)S(1)} %convolution_convert_fusion.3, bf16[16,16,32,128]{3,2,1,0:T(8,128)(2,1)} %param.8), kind=kOutput, calls=%fused_computation.78 | convolution fusion | flops 8388608 | bytes 2622464 | tf_op jit(solution)/shard_map/qj,jcrw->qrcw/dot_general | solution.py:18
  7.9 1.1 %copy.98 = bf16[4,16,32,128]{3,1,2,0:T(8,128)(2,1)} copy(bf16[4,16,32,128]{3,0,2,1:T(4,128)(2,1)S(1)} %fusion.33) | data formatting | bytes 1048576 | tf_op jit(solution)/shard_map/qj,jcrw->qrcw/dot_general | solution.py:18
  9.0 2.7 %collective-permute-start = (bf16[4,32,16,128]{3,2,1,0:T(8,128)(2,1)}, bf16[4,32,16,128]{3,2,1,0:T(8,128)(2,1)}, u32[]{:S(2)}, u32[]{:S(2)}) collective-permute-start(bf16[4,32,16,128]{3,2,1,0:T(8,128)(2,1)} %bitcast.143), channel_id=1, source_target_pairs={{0,4},{4,8},{8,12},{12,0},{1,5},{5,9},{9,13},{13,1},{2,6},{6,10},{... | collective-permute-start | bytes 1572872 | tf_op jit(solution)/shard_map/ppermute | solution.py:159
  11.7 1.3 %fusion.32 = bf16[4,16,32,128]{3,0,2,1:T(4,128)(2,1)S(1)} fusion(bf16[4,4,16]{2,1,0:T(4,128)(2,1)S(1)} %convolution_convert_fusion.3, bf16[16,16,32,128]{3,2,1,0:T(8,128)(2,1)S(1)} %copy-done.2), kind=kOutput, calls=%fused_computation.76 | convolution fusion | flops 8388608 | bytes 2622464 | tf_op jit(solution)/shard_map/qj,jcrw->qrcw/dot_general | solution.py:18
  13.0 1.1 %copy.99 = bf16[4,16,32,128]{3,1,2,0:T(8,128)(2,1)} copy(bf16[4,16,32,128]{3,0,2,1:T(4,128)(2,1)S(1)} %fusion.32) | data formatting | bytes 1048576 | tf_op jit(solution)/shard_map/qj,jcrw->qrcw/dot_general | solution.py:18
  14.1 2.6 %collective-permute-start.1 = (bf16[4,32,16,128]{3,2,1,0:T(8,128)(2,1)}, bf16[4,32,16,128]{3,2,1,0:T(8,128)(2,1)}, u32[]{:S(2)}, u32[]{:S(2)}) collective-permute-start(bf16[4,32,16,128]{3,2,1,0:T(8,128)(2,1)} %bitcast.144), channel_id=1, source_target_pairs={{0,8},{4,12},{8,0},{12,4},{1,9},{5,13},{9,1},{13,5},{2,10},{6,14},... | collective-permute-start | bytes 1572872 | tf_op jit(solution)/shard_map/ppermute | solution.py:159
  16.7 1.3 %fusion.31 = bf16[4,16,32,128]{3,0,2,1:T(4,128)(2,1)S(1)} fusion(bf16[4,4,16]{2,1,0:T(4,128)(2,1)S(1)} %convolution_convert_fusion.3, bf16[16,16,32,128]{3,2,1,0:T(8,128)(2,1)S(1)} %copy-done.2), kind=kOutput, calls=%fused_computation.74 | convolution fusion | flops 8388608 | bytes 2622464 | tf_op jit(solution)/shard_map/qj,jcrw->qrcw/dot_general | solution.py:18
  18.1 1.1 %copy.100 = bf16[4,16,32,128]{3,1,2,0:T(8,128)(2,1)} copy(bf16[4,16,32,128]{3,0,2,1:T(4,128)(2,1)S(1)} %fusion.31) | data formatting | bytes 1048576 | tf_op jit(solution)/shard_map/qj,jcrw->qrcw/dot_general | solution.py:18
  19.2 1.3 %collective-permute-start.2 = (bf16[4,32,16,128]{3,2,1,0:T(8,128)(2,1)}, bf16[4,32,16,128]{3,2,1,0:T(8,128)(2,1)}, u32[]{:S(2)}, u32[]{:S(2)}) collective-permute-start(bf16[4,32,16,128]{3,2,1,0:T(8,128)(2,1)} %bitcast.145), channel_id=1, source_target_pairs={{0,12},{4,0},{8,4},{12,8},{1,13},{5,1},{9,5},{13,9},{2,14},{6,2},{... | collective-permute-start | bytes 1572872 | tf_op jit(solution)/shard_map/ppermute | solution.py:159
  20.6 0.2 select_reduce_fusion
  20.8 0.6 and_select_fusion
  21.3 0.5 and_select_fusion.1
  22.1 0.6 compare_bitcast_fusion
  22.7 0.5 broadcast_select_fusion
  23.2 1.3 %fusion.34 = bf16[4,16,32,128]{3,0,2,1:T(4,128)(2,1)S(1)} fusion(bf16[4,4,16]{2,1,0:T(4,128)(2,1)S(1)} %convolution_convert_fusion.3, bf16[16,16,32,128]{3,2,1,0:T(8,128)(2,1)S(1)} %copy-done.2), kind=kOutput, calls=%fused_computation.80 | convolution fusion | flops 8388608 | bytes 2622464 | tf_op jit(solution)/shard_map/qj,jcrw->qrcw/dot_general | solution.py:18
  24.5 2.0 %slice.79 = bf16[16,16,32,3]{3,2,1,0:T(8,128)(2,1)} slice(bf16[16,16,32,128]{3,2,1,0:T(8,128)(2,1)S(1)} %copy-done.2), slice={[0:16], [0:16], [0:32], [125:128]} | slice | bytes 98304 | tf_op jit(solution)/shard_map/slice | solution.py:169
  26.5 3.1 %copy.74 = bf16[16,16,32,3]{2,0,3,1:T(8,128)(2,1)S(1)} copy(bf16[16,16,32,3]{3,2,1,0:T(8,128)(2,1)} %slice.79) | data formatting | bytes 98304
  29.6 0.2 fusion.1
  29.9 7.6 %all_gather.3.refs_8_ = bf16[512,512]{1,0:T(8,128)(2,1)S(1)} all-gather(bf16[512,128]{1,0:T(8,128)(2,1)S(1)} %copy-done.5), channel_id=1, replica_groups=mesh['ens'=2,'space'=4,'chan'=2,'sub'=2] {'chan','sub'}, dimensions={1}, use_global_device_ids=true | all-gather | bytes 655360 | tf_op jit(solution)/shard_map/all_gather | solution.py:181
  37.6 0.4 copy.59
  38.1 0.2 fusion
  38.5 0.7 copy.61
  39.1 0.2 pad_maximum_fusion
  39.3 2.6 %copy.62 = bf16[4,35,16,8,3]{2,0,4,3,1:T(4,128)(2,1)S(1)} copy(bf16[4,35,16,8,3]{1,3,4,2,0:T(8,128)(2,1)S(1)} %pad_maximum_fusion) | data formatting | bytes 215040 | tf_op jit(solution)/shard_map/concatenate | solution.py:171
  42.0 1.3 %copy.73 = bf16[4,7,16,120]{3,2,1,0:T(8,128)(2,1)S(1)} copy(bf16[4,7,16,120]{2,0,3,1:T(4,128)(2,1)S(1)} %bitcast.149) | data formatting | bytes 215040 | tf_op jit(solution)/shard_map/reshape | solution.py:177
  43.4 0.7 slice_bitcast_fusion.2
  44.1 0.7 collective-permute-start.4
  44.8 0.4 copy.64
  45.2 0.8 copy.75
  46.1 0.3 copy.97
  46.6 0.4 copy-done.7
  47.3 3.2 %collective-permute-start.6 = (bf16[31,16,128]{2,1,0:T(8,128)(2,1)}, bf16[31,16,128]{2,1,0:T(8,128)(2,1)}, u32[]{:S(2)}, u32[]{:S(2)}) collective-permute-start(bf16[31,16,128]{2,1,0:T(8,128)(2,1)} %get-tuple-element.12), channel_id=1, source_target_pairs={{0,12},{4,0},{8,4},{12,8},{1,13},{5,1},{9,5},{13,9},{2,14},{6,2},{... | collective-permute-start | bytes 380936 | tf_op jit(solution)/shard_map/ppermute | solution.py:159
  50.4 1.9 %collective-permute-done.4 = bf16[31,16,128]{2,1,0:T(8,128)(2,1)S(1)} collective-permute-done((bf16[31,16,128]{2,1,0:T(8,128)(2,1)S(1)}, bf16[31,16,128]{2,1,0:T(8,128)(2,1)S(1)}, u32[]{:S(2)}, u32[]{:S(2)}) %collective-permute-start.4) | collective-permute-done | bytes 127008 | tf_op jit(solution)/shard_map/ppermute | solution.py:159
  52.3 14.1 %collective-permute-start.5 = (bf16[31,16,128]{2,1,0:T(8,128)(2,1)}, bf16[31,16,128]{2,1,0:T(8,128)(2,1)}, u32[]{:S(2)}, u32[]{:S(2)}) collective-permute-start(bf16[31,16,128]{2,1,0:T(8,128)(2,1)} %get-tuple-element.13), channel_id=1, source_target_pairs={{0,8},{4,12},{8,0},{12,4},{1,9},{5,13},{9,1},{13,5},{2,10},{6,14},... | collective-permute-start | bytes 380936 | tf_op jit(solution)/shard_map/ppermute | solution.py:159
  66.4 0.5 minimum_bitcast_fusion
  67.0 0.7 stack.16.table
  67.6 5.7 %collective-permute-done.5 = bf16[31,16,128]{2,1,0:T(8,128)(2,1)} collective-permute-done((bf16[31,16,128]{2,1,0:T(8,128)(2,1)}, bf16[31,16,128]{2,1,0:T(8,128)(2,1)}, u32[]{:S(2)}, u32[]{:S(2)}) %collective-permute-start.5) | collective-permute-done | bytes 127008 | tf_op jit(solution)/shard_map/ppermute | solution.py:159
  73.3 1.1 %fusion.11.refs_4_ = bf16[31,16,128]{2,1,0:T(8,128)(2,1)S(1)} fusion(bf16[31,16,128]{2,1,0:T(8,128)(2,1)} %collective-permute-done.6, bf16[31,16,128]{2,1,0:T(8,128)(2,1)} %collective-permute-done.5, bf16[31,16,128]{2,1,0:T(8,128)(2,1)S(1)} %collective-permute-done.4, bf16[4,31,16,128]{3,2,1,0:T(8,128)(2,1)} %copy-done.4), kind=kLoop, calls=%fused_computation.23 | loop fusion | flops 507904 | bytes 634880 | tf_op jit(solution)/shard_map/convert_element_type | solution.py:184
  74.5 1.0 %copy-done = bf16[48,8,2,256]{3,1,2,0:T(8,128)(2,1)S(1)} copy-done((bf16[48,8,2,256]{3,1,2,0:T(8,128)(2,1)S(1)}, bf16[48,8,2,256]{3,1,2,0:T(8,128)(2,1)}, u32[]{:S(2)}) %copy-start) | copy-done | bytes 393240
  75.5 0.9 copy-done.1
  76.4 19.3 %shard_map.82 = bf16[8,8,32,512]{3,2,1,0:T(8,128)(2,1)} custom-call(s32[6,8]{1,0:T(8,128)S(1)} %stack.16.table, bf16[4,32,16,128]{3,2,1,0:T(8,128)(2,1)S(1)} %bitcast.147, bf16[4,32,16,128]{3,2,1,0:T(8,128)(2,1)} %collective-permute-done.refs_1_, bf16[4,32,16,128]{3,2,1,0:T(8,128)(2,1)} %collective-permute-done.1.refs_2_, ...), custom_call_target="tpu_custom_call" | custom-call | flops 8000000000 | bytes 10000000 | tf_op jit(solution)/shard_map/pallas_call | solution.py:225
  (46 shorter events, 1.8 us)
Async XLA Ops:
  1.2 10.5 %copy-start.2 = (bf16[16,16,32,128]{3,2,1,0:T(8,128)(2,1)S(1)}, bf16[16,16,32,128]{3,2,1,0:T(8,128)(2,1)}, u32[]{:S(2)}) copy-start(bf16[16,16,32,128]{3,2,1,0:T(8,128)(2,1)} %param.8) | copy-start | bytes 6291460
  1.4 36.1 %collective-permute-start.3 = (bf16[16,16,3,128]{3,0,2,1:T(8,128)(2,1)S(1)}, bf16[16,16,3,128]{3,0,2,1:T(8,128)(2,1)S(1)}, u32[]{:S(2)}, u32[]{:S(2)}) collective-permute-start(bf16[16,16,3,128]{3,0,2,1:T(8,128)(2,1)S(1)} %copy.96), channel_id=1, source_target_pairs={{0,1},{1,2},{2,3},{3,0},{4,5},{5,6},{6,7},{7,4},{8,9},{9,10},{10,1... | collective-permute-start | bytes 589832 | tf_op jit(solution)/shard_map/ppermute | solution.py:130
  9.0 65.4 %collective-permute-start = (bf16[4,32,16,128]{3,2,1,0:T(8,128)(2,1)}, bf16[4,32,16,128]{3,2,1,0:T(8,128)(2,1)}, u32[]{:S(2)}, u32[]{:S(2)}) collective-permute-start(bf16[4,32,16,128]{3,2,1,0:T(8,128)(2,1)} %bitcast.143), channel_id=1, source_target_pairs={{0,4},{4,8},{8,12},{12,0},{1,5},{5,9},{9,13},{13,1},{2,6},{6,10},{... | collective-permute-start | bytes 1572872 | tf_op jit(solution)/shard_map/ppermute | solution.py:159
  14.1 6.4 %copy-start.8 = (s32[64]{0:T(128)S(1)}, s32[64]{0:T(128)}, u32[]{:S(2)}) copy-start(s32[64]{0:T(128)} %param.9) | copy-start | bytes 772
  14.1 60.3 %collective-permute-start.1 = (bf16[4,32,16,128]{3,2,1,0:T(8,128)(2,1)}, bf16[4,32,16,128]{3,2,1,0:T(8,128)(2,1)}, u32[]{:S(2)}, u32[]{:S(2)}) collective-permute-start(bf16[4,32,16,128]{3,2,1,0:T(8,128)(2,1)} %bitcast.144), channel_id=1, source_target_pairs={{0,8},{4,12},{8,0},{12,4},{1,9},{5,13},{9,1},{13,5},{2,10},{6,14},... | collective-permute-start | bytes 1572872 | tf_op jit(solution)/shard_map/ppermute | solution.py:159
  19.2 55.2 %collective-permute-start.2 = (bf16[4,32,16,128]{3,2,1,0:T(8,128)(2,1)}, bf16[4,32,16,128]{3,2,1,0:T(8,128)(2,1)}, u32[]{:S(2)}, u32[]{:S(2)}) collective-permute-start(bf16[4,32,16,128]{3,2,1,0:T(8,128)(2,1)} %bitcast.145), channel_id=1, source_target_pairs={{0,12},{4,0},{8,4},{12,8},{1,13},{5,1},{9,5},{13,9},{2,14},{6,2},{... | collective-permute-start | bytes 1572872 | tf_op jit(solution)/shard_map/ppermute | solution.py:159
  24.5 2.0 %copy-start.6 = (bf16[3,3,16,256]{3,2,1,0:T(8,128)(2,1)S(1)}, bf16[3,3,16,256]{3,2,1,0:T(8,128)(2,1)}, u32[]{:S(2)}) copy-start(bf16[3,3,16,256]{3,2,1,0:T(8,128)(2,1)} %param.12) | copy-start | bytes 221188
  26.5 3.3 %copy-start.5 = (bf16[512,128]{1,0:T(8,128)(2,1)S(1)}, bf16[512,128]{1,0:T(8,128)(2,1)}, u32[]{:S(2)}) copy-start(bf16[512,128]{1,0:T(8,128)(2,1)} %param.14) | copy-start | bytes 393220
  43.4 1.9 %copy-start.4 = (bf16[4,31,16,128]{3,2,1,0:T(8,128)(2,1)}, bf16[4,31,16,128]{3,2,1,0:T(8,128)(2,1)S(1)}, u32[]{:S(2)}) copy-start(bf16[4,31,16,128]{3,2,1,0:T(8,128)(2,1)S(1)} %fusion.8) | copy-start | bytes 1523716
  43.4 3.0 %copy-start.3 = (bf16[3,3,256,512]{3,2,1,0:T(8,128)(2,1)S(1)}, bf16[3,3,256,512]{3,2,1,0:T(8,128)(2,1)}, u32[]{:S(2)}) copy-start(bf16[3,3,256,512]{3,2,1,0:T(8,128)(2,1)} %param.13) | copy-start | bytes 7077892
  44.1 8.2 %collective-permute-start.4 = (bf16[31,16,128]{2,1,0:T(8,128)(2,1)S(1)}, bf16[31,16,128]{2,1,0:T(8,128)(2,1)S(1)}, u32[]{:S(2)}, u32[]{:S(2)}) collective-permute-start(bf16[31,16,128]{2,1,0:T(8,128)(2,1)S(1)} %get-tuple-element.11), channel_id=1, source_target_pairs={{0,4},{4,8},{8,12},{12,0},{1,5},{5,9},{9,13},{13,1},{2,6},{6,10},{... | collective-permute-start | bytes 380936 | tf_op jit(solution)/shard_map/ppermute | solution.py:159
  46.4 0.6 copy-start.7
  46.4 0.6 copy-start.9
  46.4 0.6 copy-start.10
  47.3 20.4 %collective-permute-start.6 = (bf16[31,16,128]{2,1,0:T(8,128)(2,1)}, bf16[31,16,128]{2,1,0:T(8,128)(2,1)}, u32[]{:S(2)}, u32[]{:S(2)}) collective-permute-start(bf16[31,16,128]{2,1,0:T(8,128)(2,1)} %get-tuple-element.12), channel_id=1, source_target_pairs={{0,12},{4,0},{8,4},{12,8},{1,13},{5,1},{9,5},{13,9},{2,14},{6,2},{... | collective-permute-start | bytes 380936 | tf_op jit(solution)/shard_map/ppermute | solution.py:159
  52.3 21.0 %collective-permute-start.5 = (bf16[31,16,128]{2,1,0:T(8,128)(2,1)}, bf16[31,16,128]{2,1,0:T(8,128)(2,1)}, u32[]{:S(2)}, u32[]{:S(2)}) collective-permute-start(bf16[31,16,128]{2,1,0:T(8,128)(2,1)} %get-tuple-element.13), channel_id=1, source_target_pairs={{0,8},{4,12},{8,0},{12,4},{1,9},{5,13},{9,1},{13,5},{2,10},{6,14},... | collective-permute-start | bytes 380936 | tf_op jit(solution)/shard_map/ppermute | solution.py:159
  74.5 1.0 %copy-start = (bf16[48,8,2,256]{3,1,2,0:T(8,128)(2,1)S(1)}, bf16[48,8,2,256]{3,1,2,0:T(8,128)(2,1)}, u32[]{:S(2)}) copy-start(bf16[48,8,2,256]{3,1,2,0:T(8,128)(2,1)} %copy.75) | copy-start | bytes 1179652
  75.5 0.9 copy-start.1
